TPU v7x, 32 devices: a whole 2x2x4 slice. The times are simulated.
32 devices in a mesh: groups: 2 (over y), blk: 4 (over z), cells: 2 (over x), rep: 2 (over core).
Axes of the slice: x: 2, y: 2, z: 4, core: 2. Of those that a mesh axis runs over, the one named last changes fastest.
Arguments:
- probes: bfloat16 [32, 2, 4096], P('rep', 'cells', ('groups', 'blk')), parts along dimension 2, may hold values from -6 to 6
- depth_level: int32 [2, 4096], P('cells', ('groups', 'blk')), parts along dimension 1, may hold values from 0 to 15
- depth_scale: float32 [16], replicated, may hold values from 0.2 to 1.5
- sensitivity: bfloat16 [6, 3072, 2, 2048], P(None, ('groups', 'blk'), 'cells'), parts along dimension 1, may hold values from -0.125 to 0.125
- data_weight: float32 [6, 3072], P(None, ('groups', 'blk')), parts along dimension 1, may hold values from 0.05 to 0.5
- face_first: int32 [2, 2048], P('cells', ('groups', 'blk')), parts along dimension 1, may hold values from 0 to 2047, as said below
- face_second: int32 [2, 2048], P('cells', ('groups', 'blk')), parts along dimension 1, may hold values from 0 to 4095, as said below
- face_coef: float32 [2, 2048], P('cells', ('groups', 'blk')), parts along dimension 1, may hold values from 0.2 to 0.8
- face_count: int32 [2, 8], P('cells', ('groups', 'blk')), parts along dimension 1, may hold values from 51 to 256, as said below
Outputs:
- hessian_probe: float32 [32, 2, 4096], P('rep', 'cells', ('groups', 'blk')), parts along dimension 2
There are 2 independent parts, one for each index of `groups`. A program takes and returns all parts, laid end to end along the dimension named above; an argument that names none is the same for every part. Nothing has to cross between parts.
Inputs may be any that keep to these rules, and one draw needn't show every extreme that they name: `face_first`: a cell number within partition p. `face_second`: never equal to face_first of the same slot; values of 2048 or more name cells of the next partition, which the last partition never does. Only the first face_count[p, b] slots of block b of partition p (slots b * 256 onward) hold faces, the others are ignored; in every draw some block is full.
All inputs are finite; a program needn't handle non-finite values.
Results may differ from a plain program's by a relative error of at most 0.0029.
Values may be sent and summed in bfloat16 or wider, within the bound.
A program may use at most 64 MiB of HBM per device.

v0:
```python
import jax
import jax.numpy as jnp
from jax import lax
from jax.sharding import PartitionSpec as P


def shifted(block, axis, distance):
    devices = range(lax.axis_size(axis))
    route = [(i - distance, i) for i in devices if i - distance in devices]
    return lax.ppermute(block, axis, route)


def level_scale(depth_level, depth_scale):
    levels = jnp.arange(depth_scale.shape[0], dtype=jnp.int32)
    pick_rows = (depth_level[..., None] == levels).astype(jnp.float32)
    return jnp.sum(pick_rows * depth_scale, axis=-1)


def pick_hot(indices, offset, count):
    return (indices[:, None] - offset == jnp.arange(count, dtype=jnp.int32)[None, :]).astype(
        jnp.bfloat16
    )


def pick_values(block, hot):
    dims = (((1,), (1,)), ((), ()))
    return lax.dot_general(block, hot, dims, preferred_element_type=jnp.float32)


def spread_flux(flux, hot):
    upper = flux.astype(jnp.bfloat16)
    lower = (flux - upper.astype(jnp.float32)).astype(jnp.bfloat16)
    return jnp.dot(upper, hot, preferred_element_type=jnp.float32) + jnp.dot(
        lower, hot, preferred_element_type=jnp.float32
    )


def on_device(
    probes,
    depth_level,
    depth_scale,
    sensitivity,
    data_weight,
    face_first,
    face_second,
    face_coef,
    face_count,
):
    own_scale = level_scale(depth_level, depth_scale)
    weighted = (probes.astype(jnp.float32) * own_scale[None]).astype(jnp.bfloat16)
    probe_block = lax.all_gather(weighted, "blk", axis=2, tiled=True)
    slot_count = face_first.shape[1]
    live_all = (jnp.arange(slot_count, dtype=jnp.int32) < face_count[0, 0]).astype(jnp.float32)
    matrix = sensitivity[:, :, 0, :]
    first_cell = face_first[0]
    second_cell = face_second[0]
    coef_slots = face_coef[0]
    probe_cols = probe_block[:, 0, :]
    part_cells = probe_cols.shape[1]
    partial_value = jnp.einsum(
        "msc,qc->qms", matrix, probe_cols, preferred_element_type=jnp.float32
    )
    predicted = lax.psum(partial_value, "cells")
    residual = (data_weight[None] * predicted).astype(jnp.bfloat16)
    adjoint = jnp.einsum("msc,qms->qc", matrix, residual, preferred_element_type=jnp.float32)
    first_hot = pick_hot(first_cell, 0, part_cells)
    second_own = pick_hot(second_cell, 0, part_cells)
    first_val = pick_values(probe_cols, first_hot)
    second_val = pick_values(probe_cols, second_own)
    crossing = (second_cell >= part_cells).astype(jnp.float32)
    asked = shifted(second_cell, "cells", 1)
    asked_hot = pick_hot(asked, part_cells, part_cells)
    answer = pick_values(probe_cols, asked_hot).astype(jnp.bfloat16)
    received = shifted(answer, "cells", -1)
    second_val = second_val + crossing * received.astype(jnp.float32)
    flux_term = coef_slots * (coef_slots * live_all * (first_val - second_val))
    own_term = spread_flux(flux_term, first_hot) - spread_flux(flux_term, second_own)
    sent_flux = shifted(flux_term * crossing, "cells", 1)
    arrived = -spread_flux(sent_flux, asked_hot)
    total_term = (adjoint + own_term + arrived)[:, None, :]
    result = lax.psum_scatter(total_term, "blk", scatter_dimension=2, tiled=True)
    return result * own_scale[None]


def solution(mesh):
    return jax.shard_map(
        on_device,
        mesh=mesh,
        in_specs=(
            P("rep", "cells", ("groups", "blk")),
            P("cells", ("groups", "blk")),
            P(),
            P(None, ("groups", "blk"), "cells", None),
            P(None, ("groups", "blk")),
            P("cells", ("groups", "blk")),
            P("cells", ("groups", "blk")),
            P("cells", ("groups", "blk")),
            P("cells", ("groups", "blk")),
        ),
        out_specs=P("rep", "cells", ("groups", "blk")),
        check_vma=False,
    )
```

profile of v0, /device:TPU:0, one launch (start us, length us, event | category | flops | bytes accessed | tf_op | source)
XLA Modules:
  0.0 87.3 jit_solution(1859797593118502068)
XLA Ops:
  6.5 0.0 all-reduce.2.cloned.1.call-start
  6.5 0.8 select_reduce_fusion
  7.3 0.7 multiply_convert_fusion.2
  8.0 14.9 %all_gather.3 = bf16[16,1,2048]{2,0,1:T(8,128)(2,1)S(1)} all-gather(bf16[16,1,512]{2,0,1:T(8,128)(2,1)S(1)} %multiply_convert_fusion.2), channel_id=1, replica_groups=mesh['groups'=2,'blk'=4,'cells'=2,'rep'=2] {'blk'}, dimensions={2}, use_global_device_ids=true | all-gather | bytes 81920 | tf_op jit(solution)/shard_map/all_gather | solution.py:51
  22.9 0.0 copy-start.2
  22.9 0.0 copy-start.3
  22.9 0.0 copy-start.1
  22.9 6.9 %fusion.2 = f32[16,6,384]{2,0,1:T(8,128)} fusion(bf16[6,384,1,2048]{3,1,2,0:T(8,128)(2,1)} %param.12, bf16[16,1,2048]{2,0,1:T(8,128)(2,1)S(1)} %all_gather.3), kind=kOutput, calls=%fused_computation.2 | convolution fusion | flops 150994944 | bytes 9650176 | tf_op jit(solution)/shard_map/msc,qc->qms/dot_general | solution.py:60
  29.9 0.0 all-reduce.2.cloned.1.call-update
  29.9 0.0 copy-start
  29.9 0.0 reduce-scatter.2.cloned.1.call-start
  30.0 0.0 copy-done.2
  30.0 3.4 %collective-permute-start = (s32[256]{0:T(256)S(1)}, s32[256]{0:T(256)S(1)}, u32[]{:S(2)}, u32[]{:S(2)}) collective-permute-start(s32[256]{0:T(256)S(1)} %bitcast.33), channel_id=1, source_target_pairs={{0,2},{1,3},{4,6},{5,7},{8,10},{9,11},{12,14},{13,15},{16,18},{17,... | collective-permute-start | bytes 3080 | tf_op jit(solution)/shard_map/ppermute | solution.py:10
  33.4 0.5 fusion.15
  33.9 0.0 copy-done.3
  33.9 0.5 fusion.17
  35.0 0.0 collective-permute-done
  35.1 0.5 fusion.18
  35.5 1.3 %collective-permute-start.1 = (bf16[16,256]{1,0:T(8,128)(2,1)S(1)}, bf16[16,256]{1,0:T(8,128)(2,1)S(1)}, u32[]{:S(2)}, u32[]{:S(2)}) collective-permute-start(bf16[16,256]{1,0:T(8,128)(2,1)S(1)} %fusion.18), channel_id=1, source_target_pairs={{2,0},{3,1},{6,4},{7,5},{10,8},{11,9},{14,12},{15,13},{18,16},{19,... | collective-permute-start | bytes 24584 | tf_op jit(solution)/shard_map/ppermute | solution.py:10
  36.8 0.0 copy-done.1
  36.9 4.2 %collective-permute-done.1 = bf16[16,256]{1,0:T(8,128)(2,1)S(1)} collective-permute-done((bf16[16,256]{1,0:T(8,128)(2,1)S(1)}, bf16[16,256]{1,0:T(8,128)(2,1)S(1)}, u32[]{:S(2)}, u32[]{:S(2)}) %collective-permute-start.1) | collective-permute-done | bytes 8224 | tf_op jit(solution)/shard_map/ppermute | solution.py:10
  41.1 0.5 fusion.16
  41.6 0.5 convolution_add_fusion.2
  42.1 1.6 %collective-permute-start.2 = (f32[16,256]{1,0:T(8,128)S(1)}, f32[16,256]{1,0:T(8,128)S(1)}, u32[]{:S(2)}, u32[]{:S(2)}) collective-permute-start(f32[16,256]{1,0:T(8,128)S(1)} %get-tuple-element.5), channel_id=1, source_target_pairs={{0,2},{1,3},{4,6},{5,7},{8,10},{9,11},{12,14},{13,15},{16,18},{17,... | collective-permute-start | bytes 49160 | tf_op jit(solution)/shard_map/ppermute | solution.py:10
  43.7 0.5 fusion.14
  44.2 0.9 %collective-permute-done.2 = f32[16,256]{1,0:T(8,128)S(1)} collective-permute-done((f32[16,256]{1,0:T(8,128)S(1)}, f32[16,256]{1,0:T(8,128)S(1)}, u32[]{:S(2)}, u32[]{:S(2)}) %collective-permute-start.2) | collective-permute-done | bytes 16416 | tf_op jit(solution)/shard_map/ppermute | solution.py:10
  45.2 0.5 fusion.12
  45.7 7.2 %all-reduce.2.cloned.1.call-done = f32[16,6,384]{2,0,1:T(8,128)} async-done(((f32[16,6,384]{2,0,1:T(8,128)}), f32[16,6,384]{2,0,1:T(8,128)}) %all-reduce.2.cloned.1.call-update) | async-done | bytes 147472 | tf_op jit(solution)/shard_map/psum | solution.py:63
  52.9 0.0 copy-done
  52.9 5.1 %fusion.4 = f32[16,2048]{1,0:T(8,128)S(1)} fusion(bf16[6,384,1,2048]{3,1,2,0:T(8,128)(2,1)} %param.12, f32[16,6,384]{2,0,1:T(8,128)} %all-reduce.2.cloned.1.call-done, f32[6,384]{1,0:T(8,128)S(1)} %copy-done), kind=kOutput, calls=%fused_computation.4 | convolution fusion | flops 151068672 | bytes 9724928 | tf_op jit(solution)/shard_map/msc,qms->qc/dot_general | solution.py:65
  58.0 0.5 fusion.11
  58.5 1.1 %fusion.9 = f32[16,1,2048]{2,0,1:T(8,128)} fusion(f32[16,2048]{1,0:T(8,128)S(1)} %fusion.11, f32[16,2048]{1,0:T(8,128)S(1)} %fusion.12, s32[256]{0:T(256)S(1)} %broadcast_add_fusion, f32[16,256]{1,0:T(8,128)S(1)} %collective-permute-done.2), kind=kOutput, calls=%fused_computation.8 | convolution fusion | flops 17403904 | bytes 410624 | tf_op jit(solution)/shard_map/dot_general | solution.py:33
  59.6 0.0 reduce-scatter.2.cloned.1.call-update
  59.7 19.4 %reduce-scatter.2.cloned.1.call-done = f32[16,1,512]{2,0,1:T(8,128)} async-done(((f32[16,1,2048]{2,0,1:T(8,128)}), f32[16,1,512]{2,0,1:T(8,128)}) %reduce-scatter.2.cloned.1.call-update) | async-done | bytes 32784 | tf_op jit(solution)/shard_map/reduce_scatter | solution.py:81
  79.1 0.8 broadcast_multiply_fusion
  79.8 0.6 copy.11
  (4 shorter events, 0.0 us)
Async XLA Ops:
  6.5 46.4 %all-reduce.2.cloned.1.call-start = ((), (), s32[]{:S(2)}) async-start(), calls=%async_computation.1 | async-start | bytes 294912 | tf_op jit(solution)/shard_map/psum | solution.py:63
  22.9 7.0 %copy-start.2 = (s32[1,256]{1,0:T(1,128)S(1)}, s32[1,256]{1,0:T(1,128)}, u32[]{:S(2)}) copy-start(s32[1,256]{1,0:T(1,128)} %param.15) | copy-start | bytes 3076
  22.9 10.9 %copy-start.3 = (s32[1,256]{1,0:T(1,128)S(1)}, s32[1,256]{1,0:T(1,128)}, u32[]{:S(2)}) copy-start(s32[1,256]{1,0:T(1,128)} %param.14) | copy-start | bytes 3076
  22.9 13.9 %copy-start.1 = (f32[1,256]{1,0:T(1,128)S(1)}, f32[1,256]{1,0:T(1,128)}, u32[]{:S(2)}) copy-start(f32[1,256]{1,0:T(1,128)} %param.16) | copy-start | bytes 3076
  29.9 23.0 %copy-start = (f32[6,384]{1,0:T(8,128)S(1)}, f32[6,384]{1,0:T(8,128)}, u32[]{:S(2)}) copy-start(f32[6,384]{1,0:T(8,128)} %param.13) | copy-start | bytes 27652
  29.9 49.2 %reduce-scatter.2.cloned.1.call-start = ((), (), s32[]{:S(2)}) async-start(), calls=%async_computation.2 | async-start | bytes 163840 | tf_op jit(solution)/shard_map/reduce_scatter | solution.py:81
  30.0 5.1 %collective-permute-start = (s32[256]{0:T(256)S(1)}, s32[256]{0:T(256)S(1)}, u32[]{:S(2)}, u32[]{:S(2)}) collective-permute-start(s32[256]{0:T(256)S(1)} %bitcast.33), channel_id=1, source_target_pairs={{0,2},{1,3},{4,6},{5,7},{8,10},{9,11},{12,14},{13,15},{16,18},{17,... | collective-permute-start | bytes 3080 | tf_op jit(solution)/shard_map/ppermute | solution.py:10
  35.5 5.5 %collective-permute-start.1 = (bf16[16,256]{1,0:T(8,128)(2,1)S(1)}, bf16[16,256]{1,0:T(8,128)(2,1)S(1)}, u32[]{:S(2)}, u32[]{:S(2)}) collective-permute-start(bf16[16,256]{1,0:T(8,128)(2,1)S(1)} %fusion.18), channel_id=1, source_target_pairs={{2,0},{3,1},{6,4},{7,5},{10,8},{11,9},{14,12},{15,13},{18,16},{19,... | collective-permute-start | bytes 24584 | tf_op jit(solution)/shard_map/ppermute | solution.py:10
  42.1 3.1 %collective-permute-start.2 = (f32[16,256]{1,0:T(8,128)S(1)}, f32[16,256]{1,0:T(8,128)S(1)}, u32[]{:S(2)}, u32[]{:S(2)}) collective-permute-start(f32[16,256]{1,0:T(8,128)S(1)} %get-tuple-element.5), channel_id=1, source_target_pairs={{0,2},{1,3},{4,6},{5,7},{8,10},{9,11},{12,14},{13,15},{16,18},{17,... | collective-permute-start | bytes 49160 | tf_op jit(solution)/shard_map/ppermute | solution.py:10
Sparse Core Ops, SparseCore 0:
  30.0 22.8 all-reduce.1
  59.8 19.2 reduce-scatter.1
where the time goes:
time: 87.7 us; the launch traced here: 87.3 us
  waiting for transfers between devices  31.8 us (36%)
  matrix products  17.1 us (19%)
  blocking collectives  14.9 us (17%)
  between operations  14.1 us (16%)
  starting transfers between devices  6.36 us (7%)
  other arithmetic  2.29 us (3%)
    reduce_scatter x1, waiting for transfers between devices, on_device(): lax.psum_scatter(total_term, 'blk', scatter_dimension=2, tiled=True)  19.4 us
    all_gather x1, blocking collectives, on_device(): probe_block = lax.all_gather(weighted, 'blk', axis=2, tiled=True)  14.9 us
    psum x1, waiting for transfers between devices, on_device(): predicted = lax.psum(partial_value, 'cells')  7.25 us
    dot_general x1, matrix products, on_device(): jnp.einsum('msc,qc->qms', matrix, probe_cols, preferred_element_type=jnp....  6.94 us
    ppermute x3, starting transfers between devices, shifted(): return lax.ppermute(block, axis, route)  6.32 us
    ppermute x3, waiting for transfers between devices, shifted(): return lax.ppermute(block, axis, route)  5.15 us
    dot_general x1, matrix products, on_device(): jnp.einsum('msc,qms->qc', matrix, residual, preferred_element_type=jnp.fl...  5.1 us
    dot_general x3, matrix products, spread_flux(): jnp.dot(upper, hot, preferred_element_type=jnp.float32)  2.14 us
  transfers between devices with their start and end apart: 5, of which 4 were waited for; matrix products, arithmetic and copies ran while one was open for 4% of the time, Pallas kernels for 0%

commit v1 on v0

--- a/solution.py
+++ b/solution.py
@@ -2,6 +2,24 @@
 import jax.numpy as jnp
 from jax import lax
 from jax.sharding import PartitionSpec as P
+
+
+def joined_along(blocks, dim):
+    shape = list(blocks.shape[1:])
+    shape[dim] *= blocks.shape[0]
+    return jnp.moveaxis(blocks, 0, dim).reshape(shape)
+
+
+def grow_blocks(x, axis):
+    size = lax.axis_size(axis)
+    blocks = x[None]
+    for level in range(size.bit_length() - 1):
+        stride = 1 << level
+        partner_block = lax.ppermute(blocks, axis, [(i, i ^ stride) for i in range(size)])
+        both = jnp.stack([blocks, partner_block])
+        upper = lax.axis_index(axis) >> level & 1
+        blocks = jnp.where(upper == 0, both, both[::-1]).reshape(-1, *x.shape)
+    return blocks
 
 
 def shifted(block, axis, distance):
@@ -48,7 +66,7 @@
 ):
     own_scale = level_scale(depth_level, depth_scale)
     weighted = (probes.astype(jnp.float32) * own_scale[None]).astype(jnp.bfloat16)
-    probe_block = lax.all_gather(weighted, "blk", axis=2, tiled=True)
+    probe_block = joined_along(grow_blocks(weighted, "blk"), 2)
     slot_count = face_first.shape[1]
     live_all = (jnp.arange(slot_count, dtype=jnp.int32) < face_count[0, 0]).astype(jnp.float32)
     matrix = sensitivity[:, :, 0, :]

time: 87.7 us -> 84.6 us (0.965)
  blocking collectives: 14.9 us -> 0 us
  starting transfers between devices: 6.36 us -> 12 us
  waiting for transfers between devices: 31.8 us -> 36.4 us
  other arithmetic: 2.29 us -> 3.71 us
    all_gather x1 -> x0, blocking collectives: 14.9 us -> none  [on_device(): probe_block = lax.all_gather(weighted, 'blk', axis=2, tiled=True)]
    ppermute x0 -> x2, starting transfers between devices: none -> 5.68 us  [grow_blocks(): lax.ppermute(blocks, axis, [(i, i ^ stride) for i in range(size)])]
    psum x1, waiting for transfers between devices: 7.25 us -> 9.88 us  [on_device(): predicted = lax.psum(partial_value, 'cells')]
    ppermute x0 -> x2, waiting for transfers between devices: none -> 2.46 us  [grow_blocks(): lax.ppermute(blocks, axis, [(i, i ^ stride) for i in range(size)])]
  transfers between devices with their start and end apart: 5 -> 7, of which waited for: 4 -> 5; matrix products, arithmetic and copies ran while one was open for 4% -> 6% of each run, Pallas kernels for 0% -> 0%
where the time goes in v1:
time: 84.6 us; the launch traced here: 84.2 us
  waiting for transfers between devices  36.4 us (43%)
  matrix products  17.1 us (20%)
  between operations  14.2 us (17%)
  starting transfers between devices  12 us (14%)
  other arithmetic  3.71 us (4%)
    reduce_scatter x1, waiting for transfers between devices, on_device(): lax.psum_scatter(total_term, 'blk', scatter_dimension=2, tiled=True)  19.3 us
    psum x1, waiting for transfers between devices, on_device(): predicted = lax.psum(partial_value, 'cells')  9.88 us
    dot_general x1, matrix products, on_device(): jnp.einsum('msc,qc->qms', matrix, probe_cols, preferred_element_type=jnp....  6.91 us
    ppermute x3, starting transfers between devices, shifted(): return lax.ppermute(block, axis, route)  6.27 us
    ppermute x2, starting transfers between devices, grow_blocks(): lax.ppermute(blocks, axis, [(i, i ^ stride) for i in range(size)])  5.68 us
    dot_general x1, matrix products, on_device(): jnp.einsum('msc,qms->qc', matrix, residual, preferred_element_type=jnp.fl...  5.1 us
    ppermute x3, waiting for transfers between devices, shifted(): return lax.ppermute(block, axis, route)  4.73 us
    ppermute x2, waiting for transfers between devices, grow_blocks(): lax.ppermute(blocks, axis, [(i, i ^ stride) for i in range(size)])  2.46 us
  transfers between devices with their start and end apart: 7, of which 5 were waited for; matrix products, arithmetic and copies ran while one was open for 6% of the time, Pallas kernels for 0%

profile of v1, /device:TPU:0, one launch (start us, length us, event | category | flops | bytes accessed | tf_op | source)
XLA Modules:
  0.0 84.2 jit_solution(9420574787956643600)
XLA Ops:
  6.5 0.0 all-reduce.2.cloned.1.call-start
  6.5 0.8 select_reduce_fusion
  7.3 0.7 fusion.32
  8.0 3.0 %collective-permute-start = (bf16[1,16,1,512]{3,1,2,0:T(8,128)(2,1)S(1)}, bf16[1,16,1,512]{3,1,2,0:T(8,128)(2,1)S(1)}, u32[]{:S(2)}, u32[]{:S(2)}) collective-permute-start(bf16[1,16,1,512]{3,1,2,0:T(8,128)(2,1)S(1)} %get-tuple-element.12), channel_id=1, source_target_pairs={{0,4},{4,0},{8,12},{12,8},{1,5},{5,1},{9,13},{13,9},{2,6},{6,2},{1... | collective-permute-start | bytes 49160 | tf_op jit(solution)/shard_map/ppermute | solution.py:18
  11.1 3.4 %collective-permute-start.2 = (s32[256]{0:T(256)}, s32[256]{0:T(256)S(1)}, u32[]{:S(2)}, u32[]{:S(2)}) collective-permute-start(s32[256]{0:T(256)} %bitcast.54), channel_id=1, source_target_pairs={{0,2},{1,3},{4,6},{5,7},{8,10},{9,11},{12,14},{13,15},{16,18},{17,... | collective-permute-start | bytes 3080 | tf_op jit(solution)/shard_map/ppermute | solution.py:28
  14.5 0.7 compare_convert_fusion
  15.8 0.7 compare_select_fusion
  16.5 0.0 collective-permute-done
  16.5 2.7 %collective-permute-start.1 = (bf16[2,16,1,512]{3,1,0,2:T(8,128)(2,1)S(1)}, bf16[2,16,1,512]{3,1,0,2:T(8,128)(2,1)S(1)}, u32[]{:S(2)}, u32[]{:S(2)}) collective-permute-start(bf16[2,16,1,512]{3,1,0,2:T(8,128)(2,1)S(1)} %get-tuple-element.10), channel_id=1, source_target_pairs={{0,8},{4,12},{8,0},{12,4},{1,9},{5,13},{9,1},{13,5},{2,10},{6,14},... | collective-permute-start | bytes 98312 | tf_op jit(solution)/shard_map/ppermute | solution.py:18
  19.2 0.0 collective-permute-done.2
  19.2 2.5 %collective-permute-done.1 = bf16[2,16,1,512]{3,1,0,2:T(8,128)(2,1)S(1)} collective-permute-done((bf16[2,16,1,512]{3,1,0,2:T(8,128)(2,1)S(1)}, bf16[2,16,1,512]{3,1,0,2:T(8,128)(2,1)S(1)}, u32[]{:S(2)}, u32[]{:S(2)}) %collective-permute-start.1) | collective-permute-done | bytes 32800 | tf_op jit(solution)/shard_map/ppermute | solution.py:18
  21.7 0.1 copy.18
  21.8 0.0 copy-start.2
  21.8 0.0 copy-start.3
  21.8 6.9 %fusion.2 = f32[16,6,384]{2,0,1:T(8,128)} fusion(bf16[16,2048,1]{1,0,2:T(8,128)(2,1)S(1)} %reshape.93, bf16[6,384,1,2048]{3,1,2,0:T(8,128)(2,1)} %param.12), kind=kOutput, calls=%fused_computation.2 | convolution fusion | flops 150994944 | bytes 9650176 | tf_op jit(solution)/shard_map/msc,qc->qms/dot_general | solution.py:78
  28.7 0.0 copy-start.1
  28.7 0.0 all-reduce.2.cloned.1.call-update
  28.7 0.0 reduce-scatter.2.cloned.1.call-start
  28.8 0.0 copy-start
  28.8 0.0 copy-done.2
  28.8 0.5 fusion.15
  29.3 0.5 fusion.18
  29.8 1.3 %collective-permute-start.3 = (bf16[16,256]{1,0:T(8,128)(2,1)S(1)}, bf16[16,256]{1,0:T(8,128)(2,1)S(1)}, u32[]{:S(2)}, u32[]{:S(2)}) collective-permute-start(bf16[16,256]{1,0:T(8,128)(2,1)S(1)} %fusion.18), channel_id=1, source_target_pairs={{2,0},{3,1},{6,4},{7,5},{10,8},{11,9},{14,12},{15,13},{18,16},{19,... | collective-permute-start | bytes 24584 | tf_op jit(solution)/shard_map/ppermute | solution.py:28
  31.1 0.0 copy-done.3
  31.1 0.5 fusion.17
  31.6 3.8 %collective-permute-done.3 = bf16[16,256]{1,0:T(8,128)(2,1)S(1)} collective-permute-done((bf16[16,256]{1,0:T(8,128)(2,1)S(1)}, bf16[16,256]{1,0:T(8,128)(2,1)S(1)}, u32[]{:S(2)}, u32[]{:S(2)}) %collective-permute-start.3) | collective-permute-done | bytes 8224 | tf_op jit(solution)/shard_map/ppermute | solution.py:28
  35.4 0.0 copy-done.1
  35.4 0.5 fusion.16
  35.9 0.5 convolution_add_fusion.2
  36.4 1.6 %collective-permute-start.4 = (f32[16,256]{1,0:T(8,128)S(1)}, f32[16,256]{1,0:T(8,128)S(1)}, u32[]{:S(2)}, u32[]{:S(2)}) collective-permute-start(f32[16,256]{1,0:T(8,128)S(1)} %get-tuple-element.5), channel_id=1, source_target_pairs={{0,2},{1,3},{4,6},{5,7},{8,10},{9,11},{12,14},{13,15},{16,18},{17,... | collective-permute-start | bytes 49160 | tf_op jit(solution)/shard_map/ppermute | solution.py:28
  38.0 0.5 fusion.14
  38.5 0.9 %collective-permute-done.4 = f32[16,256]{1,0:T(8,128)S(1)} collective-permute-done((f32[16,256]{1,0:T(8,128)S(1)}, f32[16,256]{1,0:T(8,128)S(1)}, u32[]{:S(2)}, u32[]{:S(2)}) %collective-permute-start.4) | collective-permute-done | bytes 16416 | tf_op jit(solution)/shard_map/ppermute | solution.py:28
  39.4 0.5 fusion.12
  39.9 9.9 %all-reduce.2.cloned.1.call-done = f32[16,6,384]{2,0,1:T(8,128)} async-done(((f32[16,6,384]{2,0,1:T(8,128)}), f32[16,6,384]{2,0,1:T(8,128)}) %all-reduce.2.cloned.1.call-update) | async-done | bytes 147472 | tf_op jit(solution)/shard_map/psum | solution.py:81
  49.8 0.0 copy-done
  49.8 5.1 %fusion.4 = f32[16,2048]{1,0:T(8,128)S(1)} fusion(bf16[6,384,1,2048]{3,1,2,0:T(8,128)(2,1)} %param.12, f32[16,6,384]{2,0,1:T(8,128)} %all-reduce.2.cloned.1.call-done, f32[6,384]{1,0:T(8,128)S(1)} %copy-done), kind=kOutput, calls=%fused_computation.4 | convolution fusion | flops 151068672 | bytes 9724928 | tf_op jit(solution)/shard_map/msc,qms->qc/dot_general | solution.py:83
  54.9 0.5 fusion.11
  55.4 1.1 %fusion.9 = f32[16,1,2048]{2,0,1:T(8,128)} fusion(f32[16,2048]{1,0:T(8,128)S(1)} %fusion.11, f32[16,2048]{1,0:T(8,128)S(1)} %fusion.12, s32[256]{0:T(256)S(1)} %broadcast_add_fusion, f32[16,256]{1,0:T(8,128)S(1)} %collective-permute-done.4), kind=kOutput, calls=%fused_computation.8 | convolution fusion | flops 17403904 | bytes 410624 | tf_op jit(solution)/shard_map/dot_general | solution.py:51
  56.6 0.0 reduce-scatter.2.cloned.1.call-update
  56.6 19.3 %reduce-scatter.2.cloned.1.call-done = f32[16,1,512]{2,0,1:T(8,128)} async-done(((f32[16,1,2048]{2,0,1:T(8,128)}), f32[16,1,512]{2,0,1:T(8,128)}) %reduce-scatter.2.cloned.1.call-update) | async-done | bytes 32784 | tf_op jit(solution)/shard_map/reduce_scatter | solution.py:99
  75.9 0.8 broadcast_multiply_fusion
  76.7 0.6 copy.14
  (8 shorter events, 0.1 us)
Async XLA Ops:
  6.5 43.3 %all-reduce.2.cloned.1.call-start = ((), (), s32[]{:S(2)}) async-start(), calls=%async_computation.1 | async-start | bytes 294912 | tf_op jit(solution)/shard_map/psum | solution.py:81
  8.0 8.5 %collective-permute-start = (bf16[1,16,1,512]{3,1,2,0:T(8,128)(2,1)S(1)}, bf16[1,16,1,512]{3,1,2,0:T(8,128)(2,1)S(1)}, u32[]{:S(2)}, u32[]{:S(2)}) collective-permute-start(bf16[1,16,1,512]{3,1,2,0:T(8,128)(2,1)S(1)} %get-tuple-element.12), channel_id=1, source_target_pairs={{0,4},{4,0},{8,12},{12,8},{1,5},{5,1},{9,13},{13,9},{2,6},{6,2},{1... | collective-permute-start | bytes 49160 | tf_op jit(solution)/shard_map/ppermute | solution.py:18
  11.1 8.1 %collective-permute-start.2 = (s32[256]{0:T(256)}, s32[256]{0:T(256)S(1)}, u32[]{:S(2)}, u32[]{:S(2)}) collective-permute-start(s32[256]{0:T(256)} %bitcast.54), channel_id=1, source_target_pairs={{0,2},{1,3},{4,6},{5,7},{8,10},{9,11},{12,14},{13,15},{16,18},{17,... | collective-permute-start | bytes 3080 | tf_op jit(solution)/shard_map/ppermute | solution.py:28
  16.5 5.1 %collective-permute-start.1 = (bf16[2,16,1,512]{3,1,0,2:T(8,128)(2,1)S(1)}, bf16[2,16,1,512]{3,1,0,2:T(8,128)(2,1)S(1)}, u32[]{:S(2)}, u32[]{:S(2)}) collective-permute-start(bf16[2,16,1,512]{3,1,0,2:T(8,128)(2,1)S(1)} %get-tuple-element.10), channel_id=1, source_target_pairs={{0,8},{4,12},{8,0},{12,4},{1,9},{5,13},{9,1},{13,5},{2,10},{6,14},... | collective-permute-start | bytes 98312 | tf_op jit(solution)/shard_map/ppermute | solution.py:18
  21.8 7.0 %copy-start.2 = (s32[1,256]{1,0:T(1,128)S(1)}, s32[1,256]{1,0:T(1,128)}, u32[]{:S(2)}) copy-start(s32[1,256]{1,0:T(1,128)} %param.15) | copy-start | bytes 3076
  21.8 9.3 %copy-start.3 = (s32[1,256]{1,0:T(1,128)S(1)}, s32[1,256]{1,0:T(1,128)}, u32[]{:S(2)}) copy-start(s32[1,256]{1,0:T(1,128)} %param.14) | copy-start | bytes 3076
  28.7 6.7 %copy-start.1 = (f32[1,256]{1,0:T(1,128)S(1)}, f32[1,256]{1,0:T(1,128)}, u32[]{:S(2)}) copy-start(f32[1,256]{1,0:T(1,128)} %param.16) | copy-start | bytes 3076
  28.7 47.2 %reduce-scatter.2.cloned.1.call-start = ((), (), s32[]{:S(2)}) async-start(), calls=%async_computation.2 | async-start | bytes 163840 | tf_op jit(solution)/shard_map/reduce_scatter | solution.py:99
  28.8 21.0 %copy-start = (f32[6,384]{1,0:T(8,128)S(1)}, f32[6,384]{1,0:T(8,128)}, u32[]{:S(2)}) copy-start(f32[6,384]{1,0:T(8,128)} %param.13) | copy-start | bytes 27652
  29.8 5.6 %collective-permute-start.3 = (bf16[16,256]{1,0:T(8,128)(2,1)S(1)}, bf16[16,256]{1,0:T(8,128)(2,1)S(1)}, u32[]{:S(2)}, u32[]{:S(2)}) collective-permute-start(bf16[16,256]{1,0:T(8,128)(2,1)S(1)} %fusion.18), channel_id=1, source_target_pairs={{2,0},{3,1},{6,4},{7,5},{10,8},{11,9},{14,12},{15,13},{18,16},{19,... | collective-permute-start | bytes 24584 | tf_op jit(solution)/shard_map/ppermute | solution.py:28
  36.4 3.0 %collective-permute-start.4 = (f32[16,256]{1,0:T(8,128)S(1)}, f32[16,256]{1,0:T(8,128)S(1)}, u32[]{:S(2)}, u32[]{:S(2)}) collective-permute-start(f32[16,256]{1,0:T(8,128)S(1)} %get-tuple-element.5), channel_id=1, source_target_pairs={{0,2},{1,3},{4,6},{5,7},{8,10},{9,11},{12,14},{13,15},{16,18},{17,... | collective-permute-start | bytes 49160 | tf_op jit(solution)/shard_map/ppermute | solution.py:28
Sparse Core Ops, SparseCore 0:
  28.9 20.9 all-reduce.1
  56.7 19.1 reduce-scatter.1
